TPU v7x, 32 devices: a whole 2x2x4 slice. The times are simulated.
32 devices in a mesh: energy: 8 (over z, y), momentum: 4 (over x, core).
Axes of the slice: x: 2, y: 2, z: 4, core: 2. Of those that a mesh axis runs over, the one named last changes fastest.
Arguments:
- lesser: bfloat16 [8, 4, 2, 512, 512], P('energy', 'momentum'), may hold values from -6 to 6
- greater: bfloat16 [8, 4, 2, 512, 512], P('energy', 'momentum'), may hold values from -6 to 6
- retarded: bfloat16 [8, 4, 2, 512, 512], P('energy', 'momentum'), may hold values from -4.1875 to 4.1875
- occupation: float32 [2], replicated, may hold values from 0.1 to 2
- shift_slots: int32 [2, 2, 8], replicated, may hold values from 0 to 8, as said below
- coupling: int32 [2, 4, 4], replicated, may hold values from 1 to 8
Outputs:
- lesser_new: bfloat16 [8, 4, 2, 512, 512], P('energy', 'momentum')
- greater_new: bfloat16 [8, 4, 2, 512, 512], P('energy', 'momentum')
- retarded_new: bfloat16 [8, 4, 2, 512, 512], P('energy', 'momentum')
Inputs may be any that keep to these rules, and one draw needn't show every extreme that they name: The energies of the grid are held in slots in an order of their own, one energy a slot. Mode m has one shift, the same for all slots: shift_slots[m, 0, j] is the slot of the energy that lies that shift below the energy of slot j, shift_slots[m, 1, j] the slot of the energy as far above it, and 8 where that energy lies outside the grid.
All inputs are finite; a program needn't handle non-finite values.
Results may differ from a plain program's by a relative error of at most 0.0064.
Values may be sent and summed in bfloat16 or wider, within the bound.
A program may use at most 64 MiB of HBM per device.

v0:
```python
import jax
import jax.numpy as jnp
from jax import lax
from jax.sharding import PartitionSpec as P


def matrix_product(former, latter):
    return jnp.matmul(former, latter, preferred_element_type=jnp.float32)


def complex_product(former, latter):
    former_re = former[..., 0, :, :]
    former_im = former[..., 1, :, :]
    latter_re = latter[..., 0, :, :]
    latter_im = latter[..., 1, :, :]
    real_part = matrix_product(former_re, latter_re) - matrix_product(former_im, latter_im)
    imag_part = matrix_product(former_re, latter_im) + matrix_product(former_im, latter_re)
    return jnp.stack([real_part, imag_part], axis=-3)


def adjoint_product(former, propagator):
    former_re = former[..., 0, :, :]
    former_im = former[..., 1, :, :]
    prop_re = jnp.swapaxes(propagator[..., 0, :, :], -1, -2)
    prop_im = jnp.swapaxes(propagator[..., 1, :, :], -1, -2)
    real_part = matrix_product(former_re, prop_re) + matrix_product(former_im, prop_im)
    imag_part = matrix_product(former_im, prop_re) - matrix_product(former_re, prop_im)
    return jnp.stack([real_part, imag_part], axis=-3)


def scattering(less_part, more_part, weights, occupation, shift_slots):
    slots = less_part.shape[0]
    slot_ids = jnp.arange(slots, dtype=jnp.int32)
    picked = (shift_slots[..., None] == slot_ids).astype(jnp.float32)
    phonons = occupation[:, None, None]
    pick_less = phonons * picked[:, 0] + (phonons + 1.0) * picked[:, 1]
    pick_more = (phonons + 1.0) * picked[:, 0] + phonons * picked[:, 1]
    mixer_less = jnp.einsum("mjs,mkq->jksq", pick_less, weights, precision=lax.Precision.HIGHEST)
    mixer_more = jnp.einsum("mjs,mkq->jksq", pick_more, weights, precision=lax.Precision.HIGHEST)
    total_less = jnp.einsum(
        "jksq,sqxab->jkxab",
        mixer_less,
        less_part.astype(jnp.float32),
        precision=lax.Precision.HIGHEST,
    )
    total_more = jnp.einsum(
        "jksq,sqxab->jkxab",
        mixer_more,
        more_part.astype(jnp.float32),
        precision=lax.Precision.HIGHEST,
    )
    return (total_less, total_more)


def per_device(lesser, greater, retarded, occupation, shift_slots, coupling):
    momenta = coupling.shape[1]
    modes = coupling.shape[0]
    order = lesser.shape[3]
    factor = 1.0 / (order * 4.0 * (modes * momenta) ** 0.5)
    weights = coupling.astype(jnp.float32)
    rows_less, rows_more = (
        lax.all_to_all(lesser, "energy", split_axis=3, concat_axis=0, tiled=True),
        lax.all_to_all(greater, "energy", split_axis=3, concat_axis=0, tiled=True),
    )
    own_index = lax.axis_index("momentum")
    pieces = (
        lax.all_gather(rows_less, "momentum", axis=1, tiled=True),
        lax.all_gather(rows_more, "momentum", axis=1, tiled=True),
    )
    count = pieces[0].shape[1]
    chosen = lax.dynamic_slice(weights, (0, own_index, 0), (modes, 1, count))
    add_less, add_more = scattering(pieces[0], pieces[1], chosen, occupation, shift_slots)
    sigma_less = (add_less * factor).astype(jnp.bfloat16)
    sigma_more = (add_more * factor).astype(jnp.bfloat16)
    sigma_less, sigma_more = (
        lax.all_to_all(sigma_less, "energy", split_axis=0, concat_axis=3, tiled=True),
        lax.all_to_all(sigma_more, "energy", split_axis=0, concat_axis=3, tiled=True),
    )
    sigma_ret = ((sigma_more.astype(jnp.float32) - sigma_less.astype(jnp.float32)) * 0.5).astype(
        jnp.bfloat16
    )
    stacked = jnp.stack([sigma_less, sigma_more, sigma_ret])
    halfway = complex_product(retarded[None], stacked).astype(jnp.bfloat16)
    lesser_new = adjoint_product(halfway[0], retarded).astype(jnp.bfloat16)
    greater_new = adjoint_product(halfway[1], retarded).astype(jnp.bfloat16)
    retarded_new = (retarded.astype(jnp.float32) + complex_product(halfway[2], retarded)).astype(
        jnp.bfloat16
    )
    return (lesser_new, greater_new, retarded_new)


def solution(mesh):
    return jax.shard_map(
        per_device,
        mesh=mesh,
        in_specs=(
            P("energy", "momentum", None, None, None),
            P("energy", "momentum", None, None, None),
            P("energy", "momentum", None, None, None),
            P(),
            P(),
            P(),
        ),
        out_specs=(
            P("energy", "momentum", None, None, None),
            P("energy", "momentum", None, None, None),
            P("energy", "momentum", None, None, None),
        ),
        check_vma=False,
    )
```

profile of v0, /device:TPU:0, one launch (start us, length us, event | category | flops | bytes accessed | tf_op | source)
XLA Modules:
  0.0 179.2 jit_solution(12115761878033358903)
XLA Ops:
  7.2 0.0 all-gather.5.cloned.1.call-start
  7.2 2.3 %copy.29 = bf16[1,1,2,512,512]{4,2,1,0,3:T(2,128)(2,1)S(1)} copy(bf16[1,1,2,512,512]{4,3,2,1,0:T(8,128)(2,1)} %param.6) | data formatting | bytes 2097152 | tf_op args[0]
  9.5 33.0 %all_to_all.66 = bf16[1,1,2,512,512]{4,2,1,0,3:T(2,128)(2,1)S(1)} all-to-all(bf16[1,1,2,512,512]{4,2,1,0,3:T(2,128)(2,1)S(1)} %copy.29), channel_id=1, replica_groups=mesh['energy'=8,'momentum'=4] {'energy'}, dimensions={3} | all-to-all | bytes 2097152 | tf_op jit(solution)/shard_map/all_to_all | solution.py:62
  42.5 1.5 copy.69
  44.1 0.0 all-gather.7.cloned.1.call-start
  44.1 1.1 copy.36
  45.3 28.8 %all_to_all.67 = bf16[1,1,2,512,512]{4,2,1,0,3:T(2,128)(2,1)S(1)} all-to-all(bf16[1,1,2,512,512]{4,2,1,0,3:T(2,128)(2,1)S(1)} %copy.36), channel_id=1, replica_groups=mesh['energy'=8,'momentum'=4] {'energy'}, dimensions={3} | all-to-all | bytes 2097152 | tf_op jit(solution)/shard_map/all_to_all | solution.py:63
  74.1 1.5 copy.68
  75.7 0.7 dynamic-slice_convert_fusion
  76.4 0.1 fusion.68
  76.5 0.1 add_bitcast_fusion
  76.6 0.2 convolution_bitcast_fusion.1
  76.8 1.0 all-gather.5.cloned.1.call-done
  77.8 9.7 %fusion.15 = bf16[8,1,2,64,512]{4,0,3,2,1:T(8,128)(2,1)S(1)} fusion(bf16[8,4,1,2,64,512]{5,0,1,4,3,2:T(8,128)(2,1)} %all-gather.5.cloned.1.call-done, f32[8,8,4,1,1]{1,2,0,4,3:T(4,128)S(1)} %convolution_bitcast_fusion.1), kind=kOutput, calls=%fused_computation.24 | convolution fusion | flops 202375168 | bytes 5243904 | tf_op jit(solution)/shard_map/jksq,sqxab->jkxab/dot_general | solution.py:40
  87.4 1.3 copy.33
  88.7 5.5 %all-to-all-start.1 = ((bf16[8,1,2,64,512]{4,3,2,1,0:T(8,128)(2,1)}), bf16[8,1,2,64,512]{4,3,2,1,0:T(8,128)(2,1)S(1)}, u32[]{:S(2)}, u32[]{:S(2)}) async-start(bf16[8,1,2,64,512]{4,3,2,1,0:T(8,128)(2,1)} %copy.33), calls=%async_computation.1 | async-start | bytes 2097152 | tf_op jit(solution)/shard_map/all_to_all | solution.py:76
  94.2 0.2 convolution_bitcast_fusion
  94.4 20.0 %all-gather.7.cloned.1.call-done = bf16[8,4,1,2,64,512]{5,0,1,4,3,2:T(8,128)(2,1)} async-done(((bf16[8,1,1,2,64,512]{5,0,1,4,3,2:T(8,128)(2,1)}), bf16[8,4,1,2,64,512]{5,0,1,4,3,2:T(8,128)(2,1)}) %all-gather.7.cloned.1.call-update) | async-done | bytes 4194320 | tf_op jit(solution)/shard_map/all_gather | solution.py:68
  114.4 9.7 %fusion.18 = bf16[8,1,2,64,512]{4,0,3,2,1:T(8,128)(2,1)S(1)} fusion(bf16[8,4,1,2,64,512]{5,0,1,4,3,2:T(8,128)(2,1)} %all-gather.7.cloned.1.call-done, f32[8,8,4,1,1]{1,2,0,4,3:T(4,128)S(1)} %convolution_bitcast_fusion), kind=kOutput, calls=%fused_computation.25 | convolution fusion | flops 202375168 | bytes 5243904 | tf_op jit(solution)/shard_map/jksq,sqxab->jkxab/dot_general | solution.py:46
  124.0 1.3 copy.40
  125.3 5.5 %all-to-all-start.3 = ((bf16[8,1,2,64,512]{4,3,2,1,0:T(8,128)(2,1)}), bf16[8,1,2,64,512]{4,3,2,1,0:T(8,128)(2,1)S(1)}, u32[]{:S(2)}, u32[]{:S(2)}) async-start(bf16[8,1,2,64,512]{4,3,2,1,0:T(8,128)(2,1)} %copy.40), calls=%async_computation.3 | async-start | bytes 2097152 | tf_op jit(solution)/shard_map/all_to_all | solution.py:77
  130.8 0.1 copy.34
  130.9 0.5 copy.44
  131.5 25.5 %all-to-all-done.3 = bf16[8,1,2,64,512]{4,3,2,1,0:T(8,128)(2,1)S(1)} async-done(((bf16[8,1,2,64,512]{4,3,2,1,0:T(8,128)(2,1)}), bf16[8,1,2,64,512]{4,3,2,1,0:T(8,128)(2,1)S(1)}, u32[]{:S(2)}, u32[]{:S(2)}) %all-to-all-start.3) | async-done | bytes 1048608 | tf_op jit(solution)/shard_map/all_to_all | solution.py:77
  157.0 0.1 copy.41
  157.1 0.5 copy.45
  157.7 0.3 multiply_convert_fusion
  158.0 0.3 pad_maximum_fusion
  158.4 0.9 copy-done
  159.2 1.0 fusion.14
  160.2 1.0 fusion.13
  161.3 1.1 fusion.12
  162.3 1.1 fusion.11
  163.4 0.3 fusion.35
  163.7 0.5 fusion.36
  164.1 0.5 fusion.40
  164.6 0.5 fusion.50
  165.1 0.5 fusion.52
  165.6 0.5 fusion.46
  166.1 0.5 fusion.48
  166.6 0.5 fusion.21
  167.0 0.5 fusion.22
  167.5 0.5 fusion.29
  168.0 0.5 fusion.30
  168.5 0.5 fusion.27
  169.0 0.5 fusion.28
  169.5 1.4 fusion.4
  170.8 1.5 pad_maximum_fusion.2
  (12 shorter events, 0.1 us)
Async XLA Ops:
  7.2 70.6 %all-gather.5.cloned.1.call-start = ((), (), s32[]{:S(2)}) async-start(), calls=%async_computation.4 | async-start | bytes 5242880 | tf_op jit(solution)/shard_map/all_gather | solution.py:67
  9.5 34.6 %copy-start.1 = (bf16[1,1,2,512,512]{4,3,2,1,0:T(8,128)(2,1)S(1)}, bf16[1,1,2,512,512]{4,3,2,1,0:T(8,128)(2,1)}, u32[]{:S(2)}) copy-start(bf16[1,1,2,512,512]{4,3,2,1,0:T(8,128)(2,1)} %param.7) | copy-start | bytes 3145732
  44.1 70.3 %all-gather.7.cloned.1.call-start = ((), (), s32[]{:S(2)}) async-start(), calls=%async_computation.5 | async-start | bytes 5242880 | tf_op jit(solution)/shard_map/all_gather | solution.py:68
  45.2 30.5 %copy-start.2 = (s32[2,2,8]{2,1,0:T(2,128)S(1)}, s32[2,2,8]{2,1,0:T(2,128)}, u32[]{:S(2)}) copy-start(s32[2,2,8]{2,1,0:T(2,128)} %param.10) | copy-start | bytes 388
  45.2 31.2 %copy-start.3 = (f32[2]{0:T(128)S(1)}, f32[2]{0:T(128)}, u32[]{:S(2)}) copy-start(f32[2]{0:T(128)} %param.9) | copy-start | bytes 28
  88.7 36.6 %all-to-all-start.1 = ((bf16[8,1,2,64,512]{4,3,2,1,0:T(8,128)(2,1)}), bf16[8,1,2,64,512]{4,3,2,1,0:T(8,128)(2,1)S(1)}, u32[]{:S(2)}, u32[]{:S(2)}) async-start(bf16[8,1,2,64,512]{4,3,2,1,0:T(8,128)(2,1)} %copy.33), calls=%async_computation.1 | async-start | bytes 2097152 | tf_op jit(solution)/shard_map/all_to_all | solution.py:76
  125.3 31.7 %all-to-all-start.3 = ((bf16[8,1,2,64,512]{4,3,2,1,0:T(8,128)(2,1)}), bf16[8,1,2,64,512]{4,3,2,1,0:T(8,128)(2,1)S(1)}, u32[]{:S(2)}, u32[]{:S(2)}) async-start(bf16[8,1,2,64,512]{4,3,2,1,0:T(8,128)(2,1)} %copy.40), calls=%async_computation.3 | async-start | bytes 2097152 | tf_op jit(solution)/shard_map/all_to_all | solution.py:77
  158.0 1.2 copy-start
Sparse Core Ops, SparseCore 0:
  44.2 33.5 all-gather.4
  79.9 34.4 all-gather.6
where the time goes:
time: 180 us; the launch traced here: 179 us
  blocking collectives  61.8 us (34%)
  waiting for transfers between devices  46.5 us (26%)
  matrix products  29.6 us (16%)
  between operations  14.3 us (8%)
  local copies, waits for them, and re-layouts  11.2 us (6%)
  starting transfers between devices  11.1 us (6%)
  other arithmetic  4.65 us (3%)
    all_to_all x1, blocking collectives, per_device(): lax.all_to_all(lesser, 'energy', split_axis=3, concat_axis=0, tiled=True)  33 us
    all_to_all x1, blocking collectives, per_device(): lax.all_to_all(greater, 'energy', split_axis=3, concat_axis=0, tiled=True)  28.8 us
    all_to_all x1, waiting for transfers between devices, per_device(): lax.all_to_all(sigma_more, 'energy', split_axis=0, concat_axis=3, tiled=T...  25.5 us
    all_gather x1, waiting for transfers between devices, per_device(): lax.all_gather(rows_more, 'momentum', axis=1, tiled=True)  20 us
    dot_general x16, matrix products, matrix_product(): return jnp.matmul(former, latter, preferred_element_type=jnp.float32)  9.88 us
    dot_general x1, matrix products, scattering(): jnp.einsum('jksq,sqxab->jkxab', mixer_less, less_part.astype(jnp.float32)...  9.66 us
    dot_general x1, matrix products, scattering(): jnp.einsum('jksq,sqxab->jkxab', mixer_more, more_part.astype(jnp.float32)...  9.66 us
    all_to_all x1, starting transfers between devices, per_device(): lax.all_to_all(sigma_more, 'energy', split_axis=0, concat_axis=3, tiled=T...  5.52 us
  transfers between devices with their start and end apart: 4, of which 3 were waited for; matrix products, arithmetic and copies ran while one was open for 15% of the time, Pallas kernels for 0%

commit v1 on v0

--- a/solution.py
+++ b/solution.py
@@ -74,7 +74,12 @@
     sigma_more = (add_more * factor).astype(jnp.bfloat16)
     sigma_less, sigma_more = (
         lax.all_to_all(sigma_less, "energy", split_axis=0, concat_axis=3, tiled=True),
-        lax.all_to_all(sigma_more, "energy", split_axis=0, concat_axis=3, tiled=True),
+        jnp.concatenate(
+            lax.all_to_all(
+                jnp.stack(jnp.split(sigma_more, lax.axis_size("energy"), axis=0)), "energy", 0, 0
+            ),
+            axis=3,
+        ),
     )
     sigma_ret = ((sigma_more.astype(jnp.float32) - sigma_less.astype(jnp.float32)) * 0.5).astype(
         jnp.bfloat16

time: 180 us -> 186 us (1.033)
  local copies, waits for them, and re-layouts: 11.2 us -> 17.2 us
    unnamed x11 -> x18, local copies, waits for them, and re-layouts: 4.28 us -> 9 us
    split x0 -> x1, local copies, waits for them, and re-layouts: none -> 1.93 us  [per_device(): jnp.split(sigma_more, lax.axis_size('energy'), axis=0)]
  transfers between devices with their start and end apart: 4 -> 4, of which waited for: 3 -> 3; matrix products, arithmetic and copies ran while one was open for 15% -> 18% of each run, Pallas kernels for 0% -> 0%
where the time goes in v1:
time: 186 us; the launch traced here: 185 us
  blocking collectives  61.8 us (33%)
  waiting for transfers between devices  46.5 us (25%)
  matrix products  29.6 us (16%)
  local copies, waits for them, and re-layouts  17.2 us (9%)
  between operations  14.3 us (8%)
  starting transfers between devices  11.1 us (6%)
  other arithmetic  4.65 us (3%)
    all_to_all x1, blocking collectives, per_device(): lax.all_to_all(lesser, 'energy', split_axis=3, concat_axis=0, tiled=True)  33 us
    all_to_all x1, blocking collectives, per_device(): lax.all_to_all(greater, 'energy', split_axis=3, concat_axis=0, tiled=True)  28.8 us
    all_to_all x1, waiting for transfers between devices, per_device(): lax.all_to_all(jnp.stack(jnp.split(sigma_more, lax.axis_size('energy'), a...  25.5 us
    all_gather x1, waiting for transfers between devices, per_device(): lax.all_gather(rows_more, 'momentum', axis=1, tiled=True)  20.2 us
    dot_general x16, matrix products, matrix_product(): return jnp.matmul(former, latter, preferred_element_type=jnp.float32)  9.87 us
    dot_general x1, matrix products, scattering(): jnp.einsum('jksq,sqxab->jkxab', mixer_less, less_part.astype(jnp.float32)...  9.66 us
    dot_general x1, matrix products, scattering(): jnp.einsum('jksq,sqxab->jkxab', mixer_more, more_part.astype(jnp.float32)...  9.66 us
    unnamed x18, local copies, waits for them, and re-layouts  9 us
  transfers between devices with their start and end apart: 4, of which 3 were waited for; matrix products, arithmetic and copies ran while one was open for 18% of the time, Pallas kernels for 0%

profile of v1, /device:TPU:0, one launch (start us, length us, event | category | flops | bytes accessed | tf_op | source)
XLA Modules:
  0.0 185.2 jit_solution(14416650992935921692)
XLA Ops:
  7.2 2.3 %copy.148 = bf16[1,1,2,512,512]{4,2,1,0,3:T(2,128)(2,1)S(1)} copy(bf16[1,1,2,512,512]{4,3,2,1,0:T(8,128)(2,1)} %param.6) | data formatting | bytes 2097152 | tf_op args[0]
  9.5 33.0 %all_to_all.56 = bf16[1,1,2,512,512]{4,2,1,0,3:T(2,128)(2,1)S(1)} all-to-all(bf16[1,1,2,512,512]{4,2,1,0,3:T(2,128)(2,1)S(1)} %copy.148), channel_id=1, replica_groups=mesh['energy'=8,'momentum'=4] {'energy'}, dimensions={3} | all-to-all | bytes 2097152 | tf_op jit(solution)/shard_map/all_to_all | solution.py:62
  42.5 1.5 copy.203
  44.1 1.1 copy.155
  45.3 28.8 %all_to_all.57 = bf16[1,1,2,512,512]{4,2,1,0,3:T(2,128)(2,1)S(1)} all-to-all(bf16[1,1,2,512,512]{4,2,1,0,3:T(2,128)(2,1)S(1)} %copy.155), channel_id=1, replica_groups=mesh['energy'=8,'momentum'=4] {'energy'}, dimensions={3} | all-to-all | bytes 2097152 | tf_op jit(solution)/shard_map/all_to_all | solution.py:63
  74.1 1.5 copy.202
  75.7 0.7 dynamic-slice_convert_fusion
  77.0 0.8 all-gather.5.cloned.1.call-done
  77.8 9.7 %fusion.15 = bf16[8,1,2,64,512]{4,0,3,2,1:T(8,128)(2,1)S(1)} fusion(bf16[8,4,1,2,64,512]{5,0,1,4,3,2:T(8,128)(2,1)} %all-gather.5.cloned.1.call-done, f32[8,8,4,1,1]{1,2,0,4,3:T(4,128)S(1)} %convolution_bitcast_fusion.1), kind=kOutput, calls=%fused_computation.24 | convolution fusion | flops 202375168 | bytes 5243904 | tf_op jit(solution)/shard_map/jksq,sqxab->jkxab/dot_general | solution.py:40
  87.4 1.3 copy.152
  88.7 5.5 %all-to-all-start.1 = ((bf16[8,1,2,64,512]{4,3,2,1,0:T(8,128)(2,1)}), bf16[8,1,2,64,512]{4,3,2,1,0:T(8,128)(2,1)S(1)}, u32[]{:S(2)}, u32[]{:S(2)}) async-start(bf16[8,1,2,64,512]{4,3,2,1,0:T(8,128)(2,1)} %copy.152), calls=%async_computation.1 | async-start | bytes 2097152 | tf_op jit(solution)/shard_map/all_to_all | solution.py:76
  94.2 20.2 %all-gather.7.cloned.1.call-done = bf16[8,4,1,2,64,512]{5,0,1,4,3,2:T(8,128)(2,1)} async-done(((bf16[8,1,1,2,64,512]{5,0,1,4,3,2:T(8,128)(2,1)}), bf16[8,4,1,2,64,512]{5,0,1,4,3,2:T(8,128)(2,1)}) %all-gather.7.cloned.1.call-update) | async-done | bytes 4194320 | tf_op jit(solution)/shard_map/all_gather | solution.py:68
  114.4 9.7 %fusion.5 = bf16[8,2,64,512]{3,0,2,1:T(8,128)(2,1)S(1)} fusion(bf16[8,4,1,2,64,512]{5,0,1,4,3,2:T(8,128)(2,1)} %all-gather.7.cloned.1.call-done, f32[8,8,4,1,1]{1,2,0,4,3:T(4,128)S(1)} %convolution_bitcast_fusion), kind=kOutput, calls=%fused_computation.14 | convolution fusion | flops 202375168 | bytes 5243904 | tf_op jit(solution)/shard_map/jksq,sqxab->jkxab/dot_general | solution.py:46
  124.0 1.9 %fusion.68 = (bf16[1,2,64,512]{3,0,2,1:T(2,128)(2,1)S(1)}, bf16[1,2,64,512]{3,0,2,1:T(2,128)(2,1)S(1)}, bf16[1,2,64,512]{3,0,2,1:T(2,128)(2,1)S(1)}, bf16[1,2,64...) fusion(bf16[8,2,64,512]{3,0,2,1:T(8,128)(2,1)S(1)} %fusion.5), kind=kLoop, calls=%fused_computation.109 | loop fusion | bytes 2097152 | tf_op jit(solution)/shard_map/split | solution.py:79
  126.0 0.7 bitcast_dynamic-update-slice_fusion.7
  126.6 0.7 bitcast_dynamic-update-slice_fusion.6
  127.3 0.7 bitcast_dynamic-update-slice_fusion.5
  128.0 0.7 bitcast_dynamic-update-slice_fusion.4
  128.7 0.7 bitcast_dynamic-update-slice_fusion.3
  129.3 0.7 bitcast_dynamic-update-slice_fusion.2
  130.0 0.7 bitcast_dynamic-update-slice_fusion.1
  130.7 0.7 bitcast_dynamic-update-slice_fusion
  131.4 5.5 %all-to-all-start.3 = ((bf16[8,1,1,2,64,512]{5,4,3,2,1,0:T(8,128)(2,1)}), bf16[8,1,1,2,64,512]{5,4,3,2,1,0:T(8,128)(2,1)S(1)}, u32[]{:S(2)}, u32[]{:S(2)}) async-start(bf16[8,1,1,2,64,512]{5,4,3,2,1,0:T(8,128)(2,1)} %bitcast_dynamic-update-slice_fusion), calls=%async_computation.3 | async-start | bytes 2097152 | tf_op jit(solution)/shard_map/all_to_all | solution.py:78
  137.0 0.5 copy.162
  137.5 25.5 %all-to-all-done.3 = bf16[8,1,1,2,64,512]{5,4,3,2,1,0:T(8,128)(2,1)S(1)} async-done(((bf16[8,1,1,2,64,512]{5,4,3,2,1,0:T(8,128)(2,1)}), bf16[8,1,1,2,64,512]{5,4,3,2,1,0:T(8,128)(2,1)S(1)}, u32[]{:S(2)}, u32[]{:S(2)}) %all-to-all-start.3) | async-done | bytes 1048608 | tf_op jit(solution)/shard_map/all_to_all | solution.py:78
  163.2 0.5 copy.163
  163.7 0.3 multiply_convert_fusion
  164.1 0.3 pad_maximum_fusion
  164.4 0.9 copy-done
  165.3 1.0 fusion.14
  166.3 1.0 fusion.13
  167.3 1.1 fusion.12
  168.4 1.1 fusion.11
  169.4 0.3 fusion.32
  169.7 0.5 fusion.33
  170.2 0.5 fusion.37
  170.6 0.5 fusion.47
  171.1 0.5 fusion.49
  171.6 0.5 fusion.43
  172.1 0.5 fusion.45
  172.6 0.5 fusion.18
  173.1 0.5 fusion.19
  173.5 0.5 fusion.26
  174.0 0.5 fusion.27
  174.5 0.5 fusion.24
  175.0 0.5 fusion.25
  175.5 1.4 fusion.4
  176.9 1.5 pad_maximum_fusion.2
  (20 shorter events, 0.9 us)
Async XLA Ops:
  7.2 70.6 %all-gather.5.cloned.1.call-start = ((), (), s32[]{:S(2)}) async-start(), calls=%async_computation.4 | async-start | bytes 5242880 | tf_op jit(solution)/shard_map/all_gather | solution.py:67
  9.5 34.6 %copy-start.1 = (bf16[1,1,2,512,512]{4,3,2,1,0:T(8,128)(2,1)S(1)}, bf16[1,1,2,512,512]{4,3,2,1,0:T(8,128)(2,1)}, u32[]{:S(2)}) copy-start(bf16[1,1,2,512,512]{4,3,2,1,0:T(8,128)(2,1)} %param.7) | copy-start | bytes 3145732
  44.1 70.3 %all-gather.7.cloned.1.call-start = ((), (), s32[]{:S(2)}) async-start(), calls=%async_computation.5 | async-start | bytes 5242880 | tf_op jit(solution)/shard_map/all_gather | solution.py:68
  45.2 30.5 %copy-start.2 = (s32[2,2,8]{2,1,0:T(2,128)S(1)}, s32[2,2,8]{2,1,0:T(2,128)}, u32[]{:S(2)}) copy-start(s32[2,2,8]{2,1,0:T(2,128)} %param.10) | copy-start | bytes 388
  45.2 31.2 %copy-start.3 = (f32[2]{0:T(128)S(1)}, f32[2]{0:T(128)}, u32[]{:S(2)}) copy-start(f32[2]{0:T(128)} %param.9) | copy-start | bytes 28
  88.7 42.6 %all-to-all-start.1 = ((bf16[8,1,2,64,512]{4,3,2,1,0:T(8,128)(2,1)}), bf16[8,1,2,64,512]{4,3,2,1,0:T(8,128)(2,1)S(1)}, u32[]{:S(2)}, u32[]{:S(2)}) async-start(bf16[8,1,2,64,512]{4,3,2,1,0:T(8,128)(2,1)} %copy.152), calls=%async_computation.1 | async-start | bytes 2097152 | tf_op jit(solution)/shard_map/all_to_all | solution.py:76
  131.4 31.7 %all-to-all-start.3 = ((bf16[8,1,1,2,64,512]{5,4,3,2,1,0:T(8,128)(2,1)}), bf16[8,1,1,2,64,512]{5,4,3,2,1,0:T(8,128)(2,1)S(1)}, u32[]{:S(2)}, u32[]{:S(2)}) async-start(bf16[8,1,1,2,64,512]{5,4,3,2,1,0:T(8,128)(2,1)} %bitcast_dynamic-update-slice_fusion), calls=%async_computation.3 | async-start | bytes 2097152 | tf_op jit(solution)/shard_map/all_to_all | solution.py:78
  164.0 1.2 copy-start
Sparse Core Ops, SparseCore 0:
  44.2 33.5 all-gather.4
  79.9 34.4 all-gather.6
